TPU v7x, 32 devices: a whole 2x2x4 slice. The times are simulated.
32 devices in a mesh: groups: 2 (over x), loop: 4 (over y, core), width: 4 (over z).
Axes of the slice: x: 2, y: 2, z: 4, core: 2. Of those that a mesh axis runs over, the one named last changes fastest.
Arguments:
- inputs: bfloat16 [384, 8192], P(('groups', 'loop'), 'width'), parts along dimension 0, may hold values from -6 to 6
- gate_weight: bfloat16 [8192, 14336], P('width', 'loop'), may hold values from -0.0625 to 0.0625
- up_weight: bfloat16 [8192, 14336], P('width', 'loop'), may hold values from -0.0625 to 0.0625
- down_weight: bfloat16 [14336, 8192], P('loop', 'width'), may hold values from -0.046875 to 0.046875
- out_grad: bfloat16 [384, 8192], P(('groups', 'loop'), 'width'), parts along dimension 0, may hold values from -6 to 6
Outputs:
- output: bfloat16 [384, 8192], P(('groups', 'loop'), 'width'), parts along dimension 0
- input_grad: bfloat16 [384, 8192], P(('groups', 'loop'), 'width'), parts along dimension 0
- gate_grad: bfloat16 [16384, 14336], P(('groups', 'width'), 'loop'), parts along dimension 0
- up_grad: bfloat16 [16384, 14336], P(('groups', 'width'), 'loop'), parts along dimension 0
- down_grad: bfloat16 [28672, 8192], P(('groups', 'loop'), 'width'), parts along dimension 0
There are 2 independent parts, one for each index of `groups`. A program takes and returns all parts, laid end to end along the dimension named above; an argument that names none is the same for every part. Nothing has to cross between parts.
All inputs are finite; a program needn't handle non-finite values.
Results may differ from a plain program's by a relative error of at most 0.005.
Values may be sent and summed in bfloat16 or wider, within the bound.
No kernel may reach another device: no remote copies, remote signals or barrier semaphores. Data moves between devices by JAX's collectives and lax.ppermute only.
A program may use at most 192 MiB of HBM per device.

v0:
```python
import jax
import jax.numpy as jnp
from jax import lax
from jax.sharding import PartitionSpec as P


def contract_rows(left, right):
    return lax.dot_general(
        left, right, (((0,), (0,)), ((), ())), preferred_element_type=jnp.float32
    )


def contract_cols(left, right):
    return lax.dot_general(
        left, right, (((1,), (1,)), ((), ())), preferred_element_type=jnp.float32
    )


def shards(inputs, gate_weight, up_weight, down_weight, out_grad):
    hidden_dev = gate_weight.shape[1]
    gathered = lax.all_gather(inputs, "loop", axis=0, tiled=True)
    partial_pre = jnp.concatenate(
        [
            jnp.dot(gathered, gate_weight, preferred_element_type=jnp.float32),
            jnp.dot(gathered, up_weight, preferred_element_type=jnp.float32),
        ],
        axis=1,
    )
    summed = lax.psum(partial_pre, "width")
    gate = summed[:, :hidden_dev]
    up = summed[:, hidden_dev:]
    sig = jax.nn.sigmoid(gate)
    hidden = (gate * sig * up).astype(jnp.bfloat16)
    rows = hidden
    output = lax.psum_scatter(
        jnp.dot(rows, down_weight, preferred_element_type=jnp.float32),
        "loop",
        scatter_dimension=0,
        tiled=True,
    ).astype(jnp.bfloat16)
    piece = lax.all_gather(out_grad, "loop", axis=0, tiled=True)
    partial_grad = contract_cols(piece, down_weight)
    rows = hidden
    partial_grad, down_total = (partial_grad, contract_rows(rows, piece))
    down_grad = down_total.astype(jnp.bfloat16)
    hidden_grad = lax.psum(partial_grad, "width")
    pre_gate = (hidden_grad * up * sig * (1.0 + gate * (1.0 - sig))).astype(jnp.bfloat16)
    pre_up = (hidden_grad * gate * sig).astype(jnp.bfloat16)
    input_grad = lax.psum_scatter(
        contract_cols(pre_gate, gate_weight) + contract_cols(pre_up, up_weight),
        "loop",
        scatter_dimension=0,
        tiled=True,
    ).astype(jnp.bfloat16)
    gate_grad = contract_rows(gathered, pre_gate).astype(jnp.bfloat16)
    up_grad = contract_rows(gathered, pre_up).astype(jnp.bfloat16)
    return (output, input_grad, gate_grad, up_grad, down_grad)


def solution(mesh):
    in_specs = (
        P(("groups", "loop"), "width"),
        P("width", "loop"),
        P("width", "loop"),
        P("loop", "width"),
        P(("groups", "loop"), "width"),
    )
    out_specs = (
        P(("groups", "loop"), "width"),
        P(("groups", "loop"), "width"),
        P(("groups", "width"), "loop"),
        P(("groups", "width"), "loop"),
        P(("groups", "loop"), "width"),
    )
    return jax.shard_map(shards, mesh=mesh, in_specs=in_specs, out_specs=out_specs, check_vma=False)
```

profile of v0, /device:TPU:0, one launch (start us, length us, event | category | flops | bytes accessed | tf_op | source)
XLA Modules:
  0.0 447.5 jit_solution(2274933001281923944)
XLA Ops:
  7.2 0.0 all-reduce.3.cloned.1.call-start
  7.2 10.3 %all_gather.6 = bf16[192,2048]{1,0:T(8,128)(2,1)S(1)} all-gather(bf16[48,2048]{1,0:T(8,128)(2,1)} %param.5), channel_id=1, replica_groups=mesh['groups'=2,'loop'=4,'width'=4] {'loop'}, dimensions={0}, use_global_device_ids=true | all-gather | bytes 983040 | tf_op jit(solution)/shard_map/all_gather | solution.py:21
  17.5 0.0 copy-start.3
  17.5 6.9 %fusion.3 = f32[192,3584]{1,0:T(8,128)S(1)} fusion(bf16[192,2048]{1,0:T(8,128)(2,1)S(1)} %all_gather.6, bf16[2048,3584]{1,0:T(8,128)(2,1)} %param.7), kind=kOutput, calls=%fused_computation.12 | convolution fusion | flops 2818572288 | bytes 18219008 | tf_op jit(solution)/shard_map/dot_general | solution.py:25
  24.4 2.4 copy-done.3
  26.8 0.0 copy-start.2
  26.8 3.1 fusion.2
  29.9 0.0 copy-done.2
  29.9 8.7 %all_gather.7 = bf16[192,2048]{1,0:T(8,128)(2,1)S(1)} all-gather(bf16[48,2048]{1,0:T(8,128)(2,1)S(1)} %copy-done.2), channel_id=1, replica_groups=mesh['groups'=2,'loop'=4,'width'=4] {'loop'}, dimensions={0}, use_global_device_ids=true | all-gather | bytes 983040 | tf_op jit(solution)/shard_map/all_gather | solution.py:41
  38.7 2.9 pad_maximum_fusion
  41.5 0.0 copy-done
  41.5 11.7 %fusion.5 = f32[192,3584]{1,0:T(8,128)} fusion(bf16[192,2048]{1,0:T(8,128)(2,1)S(1)} %all_gather.7, bf16[3584,2048]{1,0:T(8,128)(2,1)} %param.8), kind=kOutput, calls=%fused_computation.14 | convolution fusion | flops 2818572288 | bytes 18219008 | tf_op jit(solution)/shard_map/dot_general | solution.py:14
  53.2 0.0 all-reduce.3.cloned.1.call-update
  53.2 0.0 reduce-scatter.3.cloned.1.call-start
  53.3 288.3 %all-reduce.3.cloned.1.call-done = (f32[192,7168]{1,0:T(8,128)}, f32[192,3584]{1,0:T(8,128)}) async-done(((f32[192,7168]{1,0:T(8,128)}, f32[192,3584]{1,0:T(8,128)}), (f32[192,7168]{1,0:T(8,128)}, f32[192,3584]{1,0:T(8,128)})) %all-reduce.3.cloned.1.call-update) | async-done | bytes 8257552 | tf_op jit(solution)/shard_map/psum | solution.py:29
  341.6 5.0 %multiply_convert_fusion = (bf16[192,3584]{1,0:T(8,128)(2,1)S(1)}, bf16[192,3584]{1,0:T(8,128)(2,1)}, bf16[192,3584]{1,0:T(8,128)(2,1)S(1)}) fusion(f32[192,3584]{1,0:T(8,128)} %get-tuple-element.11, f32[192,7168]{1,0:T(8,128)} %get-tuple-element.10), kind=kLoop, calls=%fused_computation.6 | loop fusion | flops 11010048 | bytes 12386304 | tf_op jit(solution)/shard_map/convert_element_type | solution.py:48
  346.6 9.3 %fusion.4 = f32[192,2048]{1,0:T(8,128)} fusion(bf16[192,3584]{1,0:T(8,128)(2,1)S(1)} %get-tuple-element.14, bf16[3584,2048]{1,0:T(8,128)(2,1)} %param.8), kind=kOutput, calls=%fused_computation.13 | convolution fusion | flops 2818572288 | bytes 17629184 | tf_op jit(solution)/shard_map/dot_general | solution.py:36
  355.9 0.0 reduce-scatter.3.cloned.1.call-update
  355.9 0.2 reduce-scatter.5.cloned.1.call-start
  356.2 8.5 %fusion.6 = f32[192,2048]{1,0:T(8,128)S(1)} fusion(bf16[192,3584]{1,0:T(8,128)(2,1)} %get-tuple-element.13, bf16[2048,3584]{1,0:T(8,128)(2,1)} %param.6), kind=kOutput, calls=%fused_computation.15 | convolution fusion | flops 2818572288 | bytes 17629184 | tf_op jit(solution)/shard_map/dot_general | solution.py:14
  364.7 11.2 %convolution_add_fusion = f32[192,2048]{1,0:T(8,128)} fusion(f32[192,2048]{1,0:T(8,128)S(1)} %fusion.6, bf16[192,3584]{1,0:T(8,128)(2,1)S(1)} %get-tuple-element.12, bf16[2048,3584]{1,0:T(8,128)(2,1)} %param.7), kind=kOutput, calls=%fused_computation.10 | convolution fusion | flops 2818965504 | bytes 19202048 | tf_op jit(solution)/shard_map/dot_general | solution.py:14
  375.9 0.0 reduce-scatter.5.cloned.1.call-update
  375.9 8.9 %fusion = bf16[2048,3584]{0,1:T(8,128)(2,1)} fusion(bf16[192,3584]{1,0:T(8,128)(2,1)} %get-tuple-element.13, bf16[192,2048]{1,0:T(8,128)(2,1)S(1)} %all_gather.6), kind=kOutput, calls=%fused_computation.3 | convolution fusion | flops 2825912320 | bytes 16842752 | tf_op jit(solution)/shard_map/dot_general | solution.py:8
  384.8 18.8 %copy.10 = bf16[2048,3584]{1,0:T(8,128)(2,1)} copy(bf16[2048,3584]{0,1:T(8,128)(2,1)} %fusion) | data formatting | bytes 29360128
  403.7 7.6 %fusion.1 = bf16[2048,3584]{0,1:T(8,128)(2,1)} fusion(bf16[192,3584]{1,0:T(8,128)(2,1)S(1)} %get-tuple-element.12, bf16[192,2048]{1,0:T(8,128)(2,1)S(1)} %all_gather.6), kind=kOutput, calls=%fused_computation.4 | convolution fusion | flops 2825912320 | bytes 16842752 | tf_op jit(solution)/shard_map/dot_general | solution.py:8
  411.2 0.0 copy-start.1
  411.2 18.7 %copy.11 = bf16[2048,3584]{1,0:T(8,128)(2,1)} copy(bf16[2048,3584]{0,1:T(8,128)(2,1)} %fusion.1) | data formatting | bytes 29360128
  430.0 0.0 copy-done.1
  430.0 7.6 %convolution_convert_fusion = bf16[3584,2048]{1,0:T(8,128)(2,1)} fusion(bf16[192,3584]{1,0:T(8,128)(2,1)S(1)} %get-tuple-element.14, bf16[192,2048]{1,0:T(8,128)(2,1)S(1)} %copy-done.1), kind=kOutput, calls=%fused_computation | convolution fusion | flops 2825912320 | bytes 16842752 | tf_op jit(solution)/shard_map/dot_general | solution.py:8
  437.6 0.0 reduce-scatter.3.cloned.1.call-done
  437.6 1.7 convert_element_type.31
  439.3 1.7 convert_element_type.34
  (2 shorter events, 0.0 us)
Async XLA Ops:
  7.2 334.4 %all-reduce.3.cloned.1.call-start = ((), (), s32[]{:S(2)}) async-start(), calls=%async_computation.4 | async-start | bytes 16515072 | tf_op jit(solution)/shard_map/psum | solution.py:29
  17.5 9.3 %copy-start.3 = (bf16[2048,3584]{1,0:T(8,128)(2,1)S(1)}, bf16[2048,3584]{1,0:T(8,128)(2,1)}, u32[]{:S(2)}) copy-start(bf16[2048,3584]{1,0:T(8,128)(2,1)} %param.6) | copy-start | bytes 44040196
  26.8 3.1 copy-start.2
  38.7 2.9 copy-start
  53.2 384.3 %reduce-scatter.3.cloned.1.call-start = ((), (), s32[]{:S(2)}) async-start(), calls=%async_computation.2 | async-start | bytes 1966080 | tf_op jit(solution)/shard_map/reduce_scatter | solution.py:35
  355.9 83.3 %reduce-scatter.5.cloned.1.call-start = ((), (), s32[]{:S(2)}) async-start(), calls=%async_computation.3 | async-start | bytes 1966080 | tf_op jit(solution)/shard_map/reduce_scatter | solution.py:49
  411.2 18.7 %copy-start.1 = (bf16[192,2048]{1,0:T(8,128)(2,1)S(1)}, bf16[192,2048]{1,0:T(8,128)(2,1)}, u32[]{:S(2)}) copy-start(bf16[192,2048]{1,0:T(8,128)(2,1)} %copy-done) | copy-start | bytes 2359300
Sparse Core Ops, SparseCore 0:
  53.4 288.1 all-reduce.2
  356.0 27.2 reduce-scatter.2
  385.8 28.1 reduce-scatter.4
where the time goes:
time: 449 us; the launch traced here: 447 us
  waiting for transfers between devices  288 us (64%)
  matrix products  74.8 us (17%)
  local copies, waits for them, and re-layouts  40 us (9%)
  blocking collectives  19 us (4%)
  between operations  13.8 us (3%)
  other arithmetic  11.3 us (3%)
    psum x1, waiting for transfers between devices, shards(): summed = lax.psum(partial_pre, 'width')  288 us
    unnamed x10, local copies, waits for them, and re-layouts  40 us
    dot_general x3, matrix products, contract_cols(): lax.dot_general(left, right, (((1,), (1,)), ((), ())), preferred_element_...  31.4 us
    dot_general x3, matrix products, contract_rows(): lax.dot_general(left, right, (((0,), (0,)), ((), ())), preferred_element_...  24.1 us
    all_gather x1, blocking collectives, shards(): gathered = lax.all_gather(inputs, 'loop', axis=0, tiled=True)  10.3 us
    dot_general x1, matrix products, shards(): jnp.dot(rows, down_weight, preferred_element_type=jnp.float32)  9.33 us
  transfers between devices with their start and end apart: 3, of which 1 were waited for; matrix products, arithmetic and copies ran while one was open for 19% of the time, Pallas kernels for 0%

commit v1 on v0

v1 whole, which is shorter than its diff:
```python
import functools

import jax
import jax.numpy as jnp
from jax import lax
from jax.experimental import pallas as pl
from jax.experimental.pallas import tpu as pltpu
from jax.sharding import PartitionSpec as P

BF16 = jnp.bfloat16
F32 = jnp.float32
LANES = 128
VMEM = 40 * 1024 * 1024


def contract_rows(left, right):
    return lax.dot_general(left, right, (((0,), (0,)), ((), ())), preferred_element_type=F32)


def contract_cols(left, right):
    return lax.dot_general(left, right, (((1,), (1,)), ((), ())), preferred_element_type=F32)


def matmul(left, right):
    return jnp.dot(left, right, preferred_element_type=F32)


def block_of(size, most):
    return max(b for b in range(LANES, most + 1, LANES) if size % b == 0)


def ring_order(n):
    return [0] + list(range(1, n, 2)) + [k for k in range(n - 1, 1, -1) if k % 2 == 0]


def ring_perm(n):
    order = ring_order(n)
    return [(order[k], order[(k + 1) % n]) for k in range(n)]


def ring_place(index, n):
    order = ring_order(n)
    place = jnp.int32(0)
    for k in range(n):
        place = jnp.where(index == order[k], k, place)
    return place.astype(jnp.int32)


def ring_gather(own, axis, perm, n):
    slots = [own]
    for _ in range(n - 1):
        slots.append(lax.ppermute(slots[-1], axis, perm))
    return slots


def ring_scatter(slots, axis, perm, n):
    total = slots[1 % n]
    for h in range(1, n):
        got = lax.ppermute(total.astype(BF16), axis, perm)
        total = got.astype(F32) + slots[(h + 1) % n]
    return total


def together(*arrays):
    return lax.optimization_barrier(list(arrays))


def params():
    return pltpu.CompilerParams(vmem_limit_bytes=VMEM)


def cost(flops, moved):
    return pl.CostEstimate(flops=flops // 8, bytes_accessed=moved // 8, transcendentals=0)


def pre_body(places, rows, gate_w, up_w, gate, up, gate_sum, up_sum):
    k = pl.program_id(1)

    @pl.when(k == 0)
    def _():
        gate_sum[...] = jnp.zeros_like(gate_sum)
        up_sum[...] = jnp.zeros_like(up_sum)

    gate_sum[...] += matmul(rows[...], gate_w[...])
    up_sum[...] += matmul(rows[...], up_w[...])

    @pl.when(k == pl.num_programs(1) - 1)
    def _():
        gate[0] = gate_sum[...].astype(gate.dtype)
        up[0] = up_sum[...].astype(up.dtype)


def partial_pre(places, rows, gate_w, up_w, shard, dtype):
    count, (tokens, depth) = places.shape[0], rows.shape
    step = block_of(depth, 512)
    weight = pl.BlockSpec((step, shard), lambda j, k, p: (k, p[j]))
    result = pl.BlockSpec((1, tokens, shard), lambda j, k, p: (j, 0, 0))
    return pl.pallas_call(
        pre_body,
        grid_spec=pltpu.PrefetchScalarGridSpec(
            num_scalar_prefetch=1,
            grid=(count, depth // step),
            in_specs=[pl.BlockSpec((tokens, step), lambda j, k, p: (0, k)), weight, weight],
            out_specs=[result, result],
            scratch_shapes=[pltpu.VMEM((tokens, shard), F32)] * 2,
        ),
        out_shape=[jax.ShapeDtypeStruct((count, tokens, shard), dtype)] * 2,
        cost_estimate=cost(4 * count * tokens * depth * shard, 4 * count * depth * shard),
        compiler_params=params(),
        name="partial_pre",
    )(places, rows, gate_w, up_w)


def grad_body(places, rows, down_w, total):
    @pl.when(pl.program_id(1) == 0)
    def _():
        total[...] = jnp.zeros_like(total)

    total[0] += contract_cols(rows[...], down_w[...])


def partial_hidden_grad(places, rows, down_w, shard):
    count, (tokens, depth) = places.shape[0], rows.shape
    step = block_of(depth, 512)
    return pl.pallas_call(
        grad_body,
        grid_spec=pltpu.PrefetchScalarGridSpec(
            num_scalar_prefetch=1,
            grid=(count, depth // step),
            in_specs=[
                pl.BlockSpec((tokens, step), lambda j, k, p: (0, k)),
                pl.BlockSpec((shard, step), lambda j, k, p: (p[j], k)),
            ],
            out_specs=pl.BlockSpec((1, tokens, shard), lambda j, k, p: (j, 0, 0)),
        ),
        out_shape=jax.ShapeDtypeStruct((count, tokens, shard), F32),
        cost_estimate=cost(2 * count * tokens * depth * shard, 2 * count * depth * shard),
        compiler_params=params(),
        name="partial_hidden_grad",
    )(places, rows, down_w)


def down_body(first, place, hidden, down_w, rows, *rest):
    if first:
        total, grad = rest
        total[...] = matmul(hidden[...], down_w[...])
    else:
        before, _, total, grad = rest
        total[...] = before[...] + matmul(hidden[...], down_w[...])
    grad[...] = contract_rows(hidden[...], rows[...]).astype(BF16)


def down_shard(place, hidden, down_w, rows, before):
    tokens, shard = hidden.shape
    units, depth = down_w.shape
    step = block_of(depth, 512)
    first = before is None
    block = pl.BlockSpec((shard, step), lambda i, p: (p[0], i))
    part = pl.BlockSpec((tokens, step), lambda i, p: (0, i))
    anywhere = pl.BlockSpec(memory_space=pl.ANY)
    return pl.pallas_call(
        functools.partial(down_body, first),
        grid_spec=pltpu.PrefetchScalarGridSpec(
            num_scalar_prefetch=1,
            grid=(depth // step,),
            in_specs=[pl.BlockSpec((tokens, shard), lambda i, p: (0, 0)), block, part]
            + ([] if first else [part, anywhere]),
            out_specs=[part, block],
        ),
        out_shape=[
            jax.ShapeDtypeStruct((tokens, depth), F32),
            jax.ShapeDtypeStruct((units, depth), BF16),
        ],
        input_output_aliases={} if first else {4: 0, 5: 1},
        cost_estimate=cost(4 * tokens * depth * shard, 4 * depth * shard),
        compiler_params=params(),
        name="down_shard",
    )(place, hidden, down_w, rows, *([] if first else before))


def input_body(first, place, pre_gate, pre_up, gate_w, up_w, *rest):
    total = rest[-1]
    value = contract_cols(pre_gate[...], gate_w[...]) + contract_cols(pre_up[...], up_w[...])
    total[...] = value if first else rest[0][...] + value


def input_shard(place, pre_gate, pre_up, gate_w, up_w, before):
    tokens, shard = pre_gate.shape
    depth = gate_w.shape[0]
    step = block_of(depth, 256)
    first = before is None
    whole = pl.BlockSpec((tokens, shard), lambda i, p: (0, 0))
    block = pl.BlockSpec((step, shard), lambda i, p: (i, p[0]))
    part = pl.BlockSpec((tokens, step), lambda i, p: (0, i))
    return pl.pallas_call(
        functools.partial(input_body, first),
        grid_spec=pltpu.PrefetchScalarGridSpec(
            num_scalar_prefetch=1,
            grid=(depth // step,),
            in_specs=[whole, whole, block, block] + ([] if first else [part]),
            out_specs=part,
        ),
        out_shape=jax.ShapeDtypeStruct((tokens, depth), F32),
        input_output_aliases={} if first else {5: 0},
        cost_estimate=cost(4 * tokens * depth * shard, 4 * depth * shard),
        compiler_params=params(),
        name="input_shard",
    )(place, pre_gate, pre_up, gate_w, up_w, *([] if first else [before]))


def weight_body(place, pre_gate, pre_up, rows, *rest):
    gate_grad, up_grad = rest[-2:]
    gate_grad[...] = contract_rows(rows[...], pre_gate[...]).astype(BF16)
    up_grad[...] = contract_rows(rows[...], pre_up[...]).astype(BF16)


def weight_shard(place, pre_gate, pre_up, rows, units, before):
    tokens, shard = pre_gate.shape
    depth = rows.shape[1]
    step = block_of(depth, 256)
    first = before is None
    whole = pl.BlockSpec((tokens, shard), lambda i, p: (0, 0))
    block = pl.BlockSpec((step, shard), lambda i, p: (i, p[0]))
    part = pl.BlockSpec((tokens, step), lambda i, p: (0, i))
    anywhere = pl.BlockSpec(memory_space=pl.ANY)
    return pl.pallas_call(
        weight_body,
        grid_spec=pltpu.PrefetchScalarGridSpec(
            num_scalar_prefetch=1,
            grid=(depth // step,),
            in_specs=[whole, whole, part] + ([] if first else [anywhere, anywhere]),
            out_specs=[block, block],
        ),
        out_shape=[jax.ShapeDtypeStruct((depth, units), BF16)] * 2,
        input_output_aliases={} if first else {4: 0, 5: 1},
        cost_estimate=cost(4 * tokens * depth * shard, 4 * depth * shard),
        compiler_params=params(),
        name="weight_shard",
    )(place, pre_gate, pre_up, rows, *([] if first else before))


def shards(loop, width, inputs, gate_weight, up_weight, down_weight, out_grad):
    hidden_dev = gate_weight.shape[1]
    shard = hidden_dev // width
    chips = loop // 2
    own_rows = inputs.shape[0]

    z_perm = ring_perm(width)
    y_perm = [(2 * a + core, 2 * b + core) for a, b in ring_perm(chips) for core in (0, 1)]
    core_perm = [(k, k ^ 1) for k in range(loop)]

    def gather_core(mine):
        return jnp.concatenate(mine + [lax.ppermute(m, "loop", core_perm) for m in mine], axis=0)

    def scatter_loop(total):
        half = chips * own_rows
        mine = total[:half] + lax.ppermute(total[half:], "loop", core_perm)
        slots = [mine[k * own_rows : (k + 1) * own_rows] for k in range(chips)]
        return ring_scatter(slots, "loop", y_perm, chips).astype(BF16)

    place = ring_place(lax.axis_index("width"), width)
    places = lax.rem(place + width - jnp.arange(width, dtype=jnp.int32), jnp.int32(width))

    def hop(sent):
        return lax.ppermute(sent, "width", z_perm)

    def add(got, term):
        return got.astype(F32) + term

    mine = ring_gather(inputs, "loop", y_perm, chips)
    out_grad, mine[-1] = together(out_grad, mine[-1])
    gathered = gather_core(mine)
    gate_1, up_1 = partial_pre(places[1:2], gathered, gate_weight, up_weight, shard, BF16)
    rest, gate_1, up_1 = together(gathered, gate_1, up_1)
    order = jnp.concatenate([places[2:], places[:1]])
    gate_n, up_n = partial_pre(order, rest, gate_weight, up_weight, shard, F32)
    piece = gather_core(ring_gather(out_grad, "loop", y_perm, chips))
    grad_n = partial_hidden_grad(places, piece, down_weight, shard)

    gate, up, sent = hop(gate_1[0]), hop(up_1[0]), grad_n[1].astype(BF16)
    sent, gate_n, up_n = together(sent, gate_n, up_n)
    for h in range(1, width - 1):
        got = hop(sent)
        gate = hop(add(gate, gate_n[h - 1]).astype(BF16))
        up = hop(add(up, up_n[h - 1]).astype(BF16))
        sent = add(got, grad_n[h + 1]).astype(BF16)
    gate, up = add(gate, gate_n[width - 2]), add(up, up_n[width - 2])
    sig = jax.nn.sigmoid(gate)
    sent, hidden_own = together(sent, (gate * sig * up).astype(BF16))
    hidden_grad = add(hop(sent), grad_n[0])
    hidden = [hidden_own, hop(hidden_own)]

    down = list(down_shard(places[:1], hidden[0], down_weight, piece, None))
    pre_gate = [(hidden_grad * up * sig * (1.0 + gate * (1.0 - sig))).astype(BF16)]
    pre_up = [(hidden_grad * gate * sig).astype(BF16)]
    total, weights = None, None
    for k in range(width):
        here = places[k : k + 1]
        if k < width - 1:
            pre_gate.append(hop(pre_gate[k]))
            pre_up.append(hop(pre_up[k]))
        total = input_shard(here, pre_gate[k], pre_up[k], gate_weight, up_weight, total)
        weights = list(weight_shard(here, pre_gate[k], pre_up[k], gathered, hidden_dev, weights))
        if k < width - 1:
            if k < width - 2:
                hidden[k + 1], down[0] = together(hidden[k + 1], down[0])
                hidden.append(hop(hidden[k + 1]))
                pre_gate[k + 1], total = together(pre_gate[k + 1], total)
                pre_up[k + 1], weights[0] = together(pre_up[k + 1], weights[0])
            down = list(down_shard(places[k + 1 : k + 2], hidden[k + 1], down_weight, piece, down))
    output = scatter_loop(down[0])
    down_grad = down[1]
    input_grad = scatter_loop(total)
    gate_grad, up_grad = weights
    return (output, input_grad, gate_grad, up_grad, down_grad)


def plain(inputs, gate_weight, up_weight, down_weight, out_grad):
    gathered = lax.all_gather(inputs, "loop", axis=0, tiled=True)
    gate = lax.psum(matmul(gathered, gate_weight), "width")
    up = lax.psum(matmul(gathered, up_weight), "width")
    sig = jax.nn.sigmoid(gate)
    hidden = (gate * sig * up).astype(BF16)
    output = lax.psum_scatter(matmul(hidden, down_weight), "loop", scatter_dimension=0, tiled=True).astype(BF16)
    piece = lax.all_gather(out_grad, "loop", axis=0, tiled=True)
    down_grad = contract_rows(hidden, piece).astype(BF16)
    hidden_grad = lax.psum(contract_cols(piece, down_weight), "width")
    pre_gate = (hidden_grad * up * sig * (1.0 + gate * (1.0 - sig))).astype(BF16)
    pre_up = (hidden_grad * gate * sig).astype(BF16)
    input_grad = lax.psum_scatter(
        contract_cols(pre_gate, gate_weight) + contract_cols(pre_up, up_weight),
        "loop",
        scatter_dimension=0,
        tiled=True,
    ).astype(BF16)
    gate_grad = contract_rows(gathered, pre_gate).astype(BF16)
    up_grad = contract_rows(gathered, pre_up).astype(BF16)
    return (output, input_grad, gate_grad, up_grad, down_grad)


def solution(mesh):
    loop, width = mesh.shape["loop"], mesh.shape["width"]

    def layer(*arrays):
        units = arrays[1].shape[1]
        if units % (width * LANES) or loop % 2 or width < 2:
            return plain(*arrays)
        return shards(loop, width, *arrays)

    in_specs = (
        P(("groups", "loop"), "width"),
        P("width", "loop"),
        P("width", "loop"),
        P("loop", "width"),
        P(("groups", "loop"), "width"),
    )
    out_specs = (
        P(("groups", "loop"), "width"),
        P(("groups", "loop"), "width"),
        P(("groups", "width"), "loop"),
        P(("groups", "width"), "loop"),
        P(("groups", "loop"), "width"),
    )
    return jax.shard_map(layer, mesh=mesh, in_specs=in_specs, out_specs=out_specs, check_vma=False)
```

time: 449 us -> 229 us (0.51)
  waiting for transfers between devices: 288 us -> 80.5 us
  Pallas kernels: 0 us -> 117 us
  matrix products: 74.8 us -> 0 us
  local copies, waits for them, and re-layouts: 40 us -> 2.91 us
  starting transfers between devices: 0.3 us -> 22.1 us
  blocking collectives: 19 us -> 0 us
  between operations: 13.8 us -> 0.93 us
  other arithmetic: 11.3 us -> 3.35 us
    psum x1 -> x0, waiting for transfers between devices: 288 us -> none  [shards(): summed = lax.psum(partial_pre, 'width')]
    pallas_call x0 -> x15, Pallas kernels: none -> 117 us  [the longest x4 31.5 us: input_shard(): pl.pallas_call(functools.partial(input_body, first), grid_spec=pltpu.Pref...]
    ppermute x0 -> x28, waiting for transfers between devices: none -> 80.5 us  [the longest x18 66.6 us: hop(): return lax.ppermute(sent, 'width', z_perm)]
    dot_general x9 -> x0, matrix products: 74.8 us -> none  [the longest x3 31.4 us: contract_cols(): lax.dot_general(left, right, (((1,), (1,)), ((), ())), preferred_element_...]
    unnamed x10 -> x6, local copies, waits for them, and re-layouts: 40 us -> 1.97 us
    ppermute x0 -> x28, starting transfers between devices: none -> 22.1 us  [the longest x18 14.4 us: hop(): return lax.ppermute(sent, 'width', z_perm)]
    all_gather x2 -> x0, blocking collectives: 19 us -> none  [the longest x1 10.3 us: shards(): gathered = lax.all_gather(inputs, 'loop', axis=0, tiled=True)]
    convert_element_type x3 -> x10, other arithmetic: 8.4 us -> 2.48 us  [the longest x2 1.43 us: scatter_loop(): return ring_scatter(slots, 'loop', y_perm, chips).astype(BF16)]
  transfers between devices with their start and end apart: 3 -> 28, of which waited for: 1 -> 15; matrix products, arithmetic and copies ran while one was open for 19% -> 2% of each run, Pallas kernels for 0% -> 52%
where the time goes in v1:
time: 229 us; the launch traced here: 227 us
  Pallas kernels  117 us (51%)
  waiting for transfers between devices  80.5 us (35%)
  starting transfers between devices  22.1 us (10%)
  other arithmetic  3.35 us (1%)
  local copies, waits for them, and re-layouts  2.91 us (1%)
    ppermute x18, waiting for transfers between devices, hop(): return lax.ppermute(sent, 'width', z_perm)  66.6 us
    pallas_call x4, Pallas kernels, input_shard(): pl.pallas_call(functools.partial(input_body, first), grid_spec=pltpu.Pref...  31.5 us
    pallas_call x4, Pallas kernels, down_shard(): pl.pallas_call(functools.partial(down_body, first), grid_spec=pltpu.Prefe...  25.4 us
    pallas_call x4, Pallas kernels, weight_shard(): pl.pallas_call(weight_body, grid_spec=pltpu.PrefetchScalarGridSpec(num_sc...  24.7 us
    pallas_call x2, Pallas kernels, partial_pre(): pl.pallas_call(pre_body, grid_spec=pltpu.PrefetchScalarGridSpec(num_scala...  20.5 us
    pallas_call x1, Pallas kernels, partial_hidden_grad(): pl.pallas_call(grad_body, grid_spec=pltpu.PrefetchScalarGridSpec(num_scal...  15.1 us
    ppermute x18, starting transfers between devices, hop(): return lax.ppermute(sent, 'width', z_perm)  14.4 us
    ppermute x2, waiting for transfers between devices, ring_scatter(): got = lax.ppermute(total.astype(BF16), axis, perm)  8.59 us
  transfers between devices with their start and end apart: 28, of which 15 were waited for; matrix products, arithmetic and copies ran while one was open for 2% of the time, Pallas kernels for 52%

profile of v1, /device:TPU:0, one launch (start us, length us, event | category | flops | bytes accessed | tf_op | source)
XLA Modules:
  0.0 227.1 jit_solution(5748033300427814000)
XLA Ops:
  0.6 3.0 %collective-permute-start = (bf16[48,2048]{1,0:T(8,128)(2,1)}, bf16[48,2048]{1,0:T(8,128)(2,1)S(1)}, u32[]{:S(2)}, u32[]{:S(2)}) collective-permute-start(bf16[48,2048]{1,0:T(8,128)(2,1)} %param.5), channel_id=1, source_target_pairs={{0,8},{4,12},{8,0},{12,4},{1,9},{5,13},{9,1},{13,5},{2,10},{6,14},... | collective-permute-start | bytes 589832 | tf_op jit(solution)/shard_map/ppermute | solution.py:52
  6.0 2.7 %collective-permute-done = bf16[48,2048]{1,0:T(8,128)(2,1)S(1)} collective-permute-done((bf16[48,2048]{1,0:T(8,128)(2,1)}, bf16[48,2048]{1,0:T(8,128)(2,1)S(1)}, u32[]{:S(2)}, u32[]{:S(2)}) %collective-permute-start) | collective-permute-done | bytes 196640 | tf_op jit(solution)/shard_map/ppermute | solution.py:52
  8.8 1.7 collective-permute-start.1
  13.3 5.8 %partial_pre.2 = (bf16[1,192,896]{2,1,0:T(8,128)(2,1)S(1)}, bf16[1,192,896]{2,1,0:T(8,128)(2,1)S(1)}) custom-call(s32[1]{0:T(128)} %get-tuple-element.92.places.place, bf16[192,2048]{1,0:T(8,128)(2,1)S(1)} %constant_dynamic-update-slice_fusion.4.rows, bf16[2048,3584]{1,0:T(8,128)(2,1)} %gate_w.11, bf16[2048,3584]{1,0:T(8,128)(2,1)} %up_w.11), custom_call_target="tpu_custom_call" | custom-call | flops 176160768 | bytes 917504 | tf_op jit(solution)/shard_map/partial_pre/pallas_call | solution.py:98
  20.7 2.6 %collective-permute-start.11 = (bf16[192,896]{1,0:T(8,128)(2,1)S(1)}, bf16[192,896]{1,0:T(8,128)(2,1)S(1)}, u32[]{:S(2)}, u32[]{:S(2)}) collective-permute-start(bf16[192,896]{1,0:T(8,128)(2,1)S(1)} %bitcast.54), channel_id=1, source_target_pairs={{0,1},{1,3},{3,2},{2,0},{4,5},{5,7},{7,6},{6,4},{8,9},{9,11},{11,1... | collective-permute-start | bytes 1032200 | tf_op jit(solution)/shard_map/ppermute | solution.py:265
  23.3 14.8 %partial_pre.3 = (f32[3,192,896]{2,1,0:T(8,128)S(1)}, f32[3,192,896]{2,1,0:T(8,128)S(1)}) custom-call(s32[3]{0:T(128)S(1)} %pad_add_fusion.places, bf16[192,2048]{1,0:T(8,128)(2,1)S(1)} %constant_dynamic-update-slice_fusion.4.rows, bf16[2048,3584]{1,0:T(8,128)(2,1)} %gate_w.11, bf16[2048,3584]{1,0:T(8,128)(2,1)} %up_w.11), custom_call_target="tpu_custom_call" | custom-call | flops 528482304 | bytes 2752512 | tf_op jit(solution)/shard_map/partial_pre/pallas_call | solution.py:98
  39.6 15.1 %partial_hidden_grad.1 = f32[4,192,896]{2,1,0:T(8,128)S(1)} custom-call(s32[4]{0:T(128)S(1)} %compare_select_fusion.places, bf16[192,2048]{1,0:T(8,128)(2,1)S(1)} %constant_dynamic-update-slice_fusion.rows, bf16[3584,2048]{1,0:T(8,128)(2,1)} %down_w.9), custom_call_target="tpu_custom_call" | custom-call | flops 352321536 | bytes 1835008 | tf_op jit(solution)/shard_map/partial_hidden_grad/pallas_call | solution.py:125
  57.5 9.2 %collective-permute-done.6 = bf16[192,896]{1,0:T(8,128)(2,1)S(1)} collective-permute-done((bf16[192,896]{1,0:T(8,128)(2,1)S(1)}, bf16[192,896]{1,0:T(8,128)(2,1)S(1)}, u32[]{:S(2)}, u32[]{:S(2)}) %collective-permute-start.6) | collective-permute-done | bytes 344096 | tf_op jit(solution)/shard_map/ppermute | solution.py:265
  66.8 7.2 %collective-permute-done.9 = bf16[192,896]{1,0:T(8,128)(2,1)S(1)} collective-permute-done((bf16[192,896]{1,0:T(8,128)(2,1)S(1)}, bf16[192,896]{1,0:T(8,128)(2,1)S(1)}, u32[]{:S(2)}, u32[]{:S(2)}) %collective-permute-start.9) | collective-permute-done | bytes 344096 | tf_op jit(solution)/shard_map/ppermute | solution.py:265
  74.2 7.2 %collective-permute-done.12 = bf16[192,896]{1,0:T(8,128)(2,1)S(1)} collective-permute-done((bf16[192,896]{1,0:T(8,128)(2,1)S(1)}, bf16[192,896]{1,0:T(8,128)(2,1)S(1)}, u32[]{:S(2)}, u32[]{:S(2)}) %collective-permute-start.12) | collective-permute-done | bytes 344096 | tf_op jit(solution)/shard_map/ppermute | solution.py:265
  81.6 7.2 %collective-permute-done.7 = bf16[192,896]{1,0:T(8,128)(2,1)S(1)} collective-permute-done((bf16[192,896]{1,0:T(8,128)(2,1)S(1)}, bf16[192,896]{1,0:T(8,128)(2,1)S(1)}, u32[]{:S(2)}, u32[]{:S(2)}) %collective-permute-start.7) | collective-permute-done | bytes 344096 | tf_op jit(solution)/shard_map/ppermute | solution.py:265
  88.9 7.3 %collective-permute-done.10 = bf16[192,896]{1,0:T(8,128)(2,1)S(1)} collective-permute-done((bf16[192,896]{1,0:T(8,128)(2,1)S(1)}, bf16[192,896]{1,0:T(8,128)(2,1)S(1)}, u32[]{:S(2)}, u32[]{:S(2)}) %collective-permute-start.10) | collective-permute-done | bytes 344096 | tf_op jit(solution)/shard_map/ppermute | solution.py:265
  96.2 6.6 %collective-permute-done.13 = bf16[192,896]{1,0:T(8,128)(2,1)S(1)} collective-permute-done((bf16[192,896]{1,0:T(8,128)(2,1)S(1)}, bf16[192,896]{1,0:T(8,128)(2,1)S(1)}, u32[]{:S(2)}, u32[]{:S(2)}) %collective-permute-start.13) | collective-permute-done | bytes 344096 | tf_op jit(solution)/shard_map/ppermute | solution.py:265
  103.9 6.3 %down_shard.4 = (f32[192,2048]{1,0:T(8,128)S(1)}, bf16[3584,2048]{1,0:T(8,128)(2,1)}) custom-call(s32[1]{0:T(128)} %get-tuple-element.93.place, bf16[192,896]{1,0:T(8,128)(2,1)S(1)} %multiply_convert_fusion.2.hidden, bf16[3584,2048]{1,0:T(8,128)(2,1)} %down_w.9, bf16[192,2048]{1,0:T(8,128)(2,1)S(1)} %constant_dynamic-update-slice_fusion.rows), custom_call_target="tpu_custom_call" | custom-call | flops 176160768 | bytes 917504 | tf_op jit(solution)/shard_map/down_shard/pallas_call | solution.py:161
  110.2 4.8 %collective-permute-done.14.hidden = bf16[192,896]{1,0:T(8,128)(2,1)S(1)} collective-permute-done((bf16[192,896]{1,0:T(8,128)(2,1)S(1)}, bf16[192,896]{1,0:T(8,128)(2,1)S(1)}, u32[]{:S(2)}, u32[]{:S(2)}) %collective-permute-start.14) | collective-permute-done | bytes 344096 | tf_op jit(solution)/shard_map/ppermute | solution.py:265
  115.0 7.4 %collective-permute-done.19 = bf16[192,896]{1,0:T(8,128)(2,1)S(1)} collective-permute-done((bf16[192,896]{1,0:T(8,128)(2,1)S(1)}, bf16[192,896]{1,0:T(8,128)(2,1)S(1)}, u32[]{:S(2)}, u32[]{:S(2)}) %collective-permute-start.19) | collective-permute-done | bytes 344096 | tf_op jit(solution)/shard_map/ppermute | solution.py:265
  123.6 6.4 %down_shard.5 = (f32[192,2048]{1,0:T(8,128)S(1)}, bf16[3584,2048]{1,0:T(8,128)(2,1)}) custom-call(s32[1]{0:T(128)} %get-tuple-element.92.places.place, bf16[192,896]{1,0:T(8,128)(2,1)S(1)} %collective-permute-done.14.hidden, bf16[3584,2048]{1,0:T(8,128)(2,1)} %down_w.9, ...), custom_call_target="tpu_custom_call", output_to_operand_aliasing={{0}: (4, {}), {1}: (5, {})} | custom-call | flops 176160768 | bytes 917504 | tf_op jit(solution)/shard_map/down_shard/pallas_call | solution.py:161
  130.8 6.2 %weight_shard.4 = (bf16[2048,3584]{1,0:T(8,128)(2,1)}, bf16[2048,3584]{1,0:T(8,128)(2,1)}) custom-call(s32[1]{0:T(128)} %get-tuple-element.93.place, bf16[192,896]{1,0:T(8,128)(2,1)S(1)} %get-tuple-element.90.pre_gate, bf16[192,896]{1,0:T(8,128)(2,1)S(1)} %get-tuple-element.89.pre_up, bf16[192,2048]{1,0:T(8,128)(2,1)S(1)} %constant_dynamic-update-slice_fusion.4.rows), custom_call_target="tpu_custom_call" | custom-call | flops 176160768 | bytes 917504 | tf_op jit(solution)/shard_map/weight_shard/pallas_call | solution.py:226
  137.0 7.8 %input_shard.4.rest_0_ = f32[192,2048]{1,0:T(8,128)S(1)} custom-call(s32[1]{0:T(128)} %get-tuple-element.93.place, bf16[192,896]{1,0:T(8,128)(2,1)S(1)} %get-tuple-element.90.pre_gate, bf16[192,896]{1,0:T(8,128)(2,1)S(1)} %get-tuple-element.89.pre_up, bf16[2048,3584]{1,0:T(8,128)(2,1)} %gate_w.11, bf16[2048,3584]{1,0:T(8,128)(2,1)} %up_w.11), custom_call_target="tpu_custom_call" | custom-call | flops 176160768 | bytes 917504 | tf_op jit(solution)/shard_map/input_shard/pallas_call | solution.py:195
  144.8 3.4 %collective-permute-start.24 = (bf16[192,896]{1,0:T(8,128)(2,1)S(1)}, bf16[192,896]{1,0:T(8,128)(2,1)S(1)}, u32[]{:S(2)}, u32[]{:S(2)}) collective-permute-start(bf16[192,896]{1,0:T(8,128)(2,1)S(1)} %collective-permute-done.22.pre_up), channel_id=1, source_target_pairs={{0,1},{1,3},{3,2},{2,0},{4,5},{5,7},{7,6},{6,4},{8,9},{9,11},{11,1... | collective-permute-start | bytes 1032200 | tf_op jit(solution)/shard_map/ppermute | solution.py:265
  148.3 6.4 %down_shard.6 = (f32[192,2048]{1,0:T(8,128)S(1)}, bf16[3584,2048]{1,0:T(8,128)(2,1)}) custom-call(s32[1]{0:T(128)} %get-tuple-element.91.place, bf16[192,896]{1,0:T(8,128)(2,1)S(1)} %collective-permute-done.15.hidden, bf16[3584,2048]{1,0:T(8,128)(2,1)} %down_w.9, ...), custom_call_target="tpu_custom_call", output_to_operand_aliasing={{0}: (4, {}), {1}: (5, {})} | custom-call | flops 176160768 | bytes 917504 | tf_op jit(solution)/shard_map/down_shard/pallas_call | solution.py:161
  154.7 6.3 %down_shard.7 = (f32[192,2048]{1,0:T(8,128)S(1)}, bf16[3584,2048]{1,0:T(8,128)(2,1)}) custom-call(s32[1]{0:T(128)} %get-tuple-element.94.place, bf16[192,896]{1,0:T(8,128)(2,1)S(1)} %collective-permute-done.16.hidden, bf16[3584,2048]{1,0:T(8,128)(2,1)} %down_w.9, ...), custom_call_target="tpu_custom_call", output_to_operand_aliasing={{0}: (4, {}), {1}: (5, {})} | custom-call | flops 176160768 | bytes 917504 | tf_op jit(solution)/shard_map/down_shard/pallas_call | solution.py:161
  161.2 7.9 %input_shard.5.rest_0_ = f32[192,2048]{1,0:T(8,128)S(1)} custom-call(s32[1]{0:T(128)} %get-tuple-element.92.places.place, bf16[192,896]{1,0:T(8,128)(2,1)S(1)} %collective-permute-done.20.pre_gate, bf16[192,896]{1,0:T(8,128)(2,1)S(1)} %collective-permute-done.22.pre_up, bf16[2048,3584]{1,0:T(8,128)(2,1)} %gate_w.11, ...), custom_call_target="tpu_custom_call", output_to_operand_aliasing={{}: (5, {})} | custom-call | flops 176160768 | bytes 917504 | tf_op jit(solution)/shard_map/input_shard/pallas_call | solution.py:195
  169.1 6.2 %weight_shard.5 = (bf16[2048,3584]{1,0:T(8,128)(2,1)}, bf16[2048,3584]{1,0:T(8,128)(2,1)}) custom-call(s32[1]{0:T(128)} %get-tuple-element.92.places.place, bf16[192,896]{1,0:T(8,128)(2,1)S(1)} %collective-permute-done.20.pre_gate, bf16[192,896]{1,0:T(8,128)(2,1)S(1)} %collective-permute-done.22.pre_up, ...), custom_call_target="tpu_custom_call", output_to_operand_aliasing={{0}: (4, {}), {1}: (5, {})} | custom-call | flops 176160768 | bytes 917504 | tf_op jit(solution)/shard_map/weight_shard/pallas_call | solution.py:226
  176.8 7.9 %input_shard.6.rest_0_ = f32[192,2048]{1,0:T(8,128)S(1)} custom-call(s32[1]{0:T(128)} %get-tuple-element.91.place, bf16[192,896]{1,0:T(8,128)(2,1)S(1)} %collective-permute-done.21.pre_gate, bf16[192,896]{1,0:T(8,128)(2,1)S(1)} %collective-permute-done.24.pre_up, bf16[2048,3584]{1,0:T(8,128)(2,1)} %gate_w.11, ...), custom_call_target="tpu_custom_call", output_to_operand_aliasing={{}: (5, {})} | custom-call | flops 176160768 | bytes 917504 | tf_op jit(solution)/shard_map/input_shard/pallas_call | solution.py:195
  184.8 2.4 %collective-permute-done.25.pre_up = bf16[192,896]{1,0:T(8,128)(2,1)S(1)} collective-permute-done((bf16[192,896]{1,0:T(8,128)(2,1)S(1)}, bf16[192,896]{1,0:T(8,128)(2,1)S(1)}, u32[]{:S(2)}, u32[]{:S(2)}) %collective-permute-start.25) | collective-permute-done | bytes 344096 | tf_op jit(solution)/shard_map/ppermute | solution.py:265
  187.2 7.1 %collective-permute-done.23.pre_gate = bf16[192,896]{1,0:T(8,128)(2,1)S(1)} collective-permute-done((bf16[192,896]{1,0:T(8,128)(2,1)S(1)}, bf16[192,896]{1,0:T(8,128)(2,1)S(1)}, u32[]{:S(2)}, u32[]{:S(2)}) %collective-permute-start.23) | collective-permute-done | bytes 344096 | tf_op jit(solution)/shard_map/ppermute | solution.py:265
  194.3 7.9 %input_shard.7 = f32[192,2048]{1,0:T(8,128)S(1)} custom-call(s32[1]{0:T(128)} %get-tuple-element.94.place, bf16[192,896]{1,0:T(8,128)(2,1)S(1)} %collective-permute-done.23.pre_gate, bf16[192,896]{1,0:T(8,128)(2,1)S(1)} %collective-permute-done.25.pre_up, bf16[2048,3584]{1,0:T(8,128)(2,1)} %gate_w.11, ...), custom_call_target="tpu_custom_call", output_to_operand_aliasing={{}: (5, {})} | custom-call | flops 176160768 | bytes 917504 | tf_op jit(solution)/shard_map/input_shard/pallas_call | solution.py:195
  202.3 6.2 %weight_shard.6 = (bf16[2048,3584]{1,0:T(8,128)(2,1)}, bf16[2048,3584]{1,0:T(8,128)(2,1)}) custom-call(s32[1]{0:T(128)} %get-tuple-element.91.place, bf16[192,896]{1,0:T(8,128)(2,1)S(1)} %collective-permute-done.21.pre_gate, bf16[192,896]{1,0:T(8,128)(2,1)S(1)} %collective-permute-done.24.pre_up, ...), custom_call_target="tpu_custom_call", output_to_operand_aliasing={{0}: (4, {}), {1}: (5, {})} | custom-call | flops 176160768 | bytes 917504 | tf_op jit(solution)/shard_map/weight_shard/pallas_call | solution.py:226
  208.5 6.2 %weight_shard.7 = (bf16[2048,3584]{1,0:T(8,128)(2,1)}, bf16[2048,3584]{1,0:T(8,128)(2,1)}) custom-call(s32[1]{0:T(128)} %get-tuple-element.94.place, bf16[192,896]{1,0:T(8,128)(2,1)S(1)} %collective-permute-done.23.pre_gate, bf16[192,896]{1,0:T(8,128)(2,1)S(1)} %collective-permute-done.25.pre_up, ...), custom_call_target="tpu_custom_call", output_to_operand_aliasing={{0}: (4, {}), {1}: (5, {})} | custom-call | flops 176160768 | bytes 917504 | tf_op jit(solution)/shard_map/weight_shard/pallas_call | solution.py:226
  217.1 5.5 %collective-permute-done.18 = bf16[48,2048]{1,0:T(8,128)(2,1)S(1)} collective-permute-done((bf16[48,2048]{1,0:T(8,128)(2,1)S(1)}, bf16[48,2048]{1,0:T(8,128)(2,1)S(1)}, u32[]{:S(2)}, u32[]{:S(2)}) %collective-permute-start.18) | collective-permute-done | bytes 196640 | tf_op jit(solution)/shard_map/ppermute | solution.py:59
  223.3 3.1 %collective-permute-done.27 = bf16[48,2048]{1,0:T(8,128)(2,1)S(1)} collective-permute-done((bf16[48,2048]{1,0:T(8,128)(2,1)S(1)}, bf16[48,2048]{1,0:T(8,128)(2,1)S(1)}, u32[]{:S(2)}, u32[]{:S(2)}) %collective-permute-start.27) | collective-permute-done | bytes 196640 | tf_op jit(solution)/shard_map/ppermute | solution.py:59
  (68 shorter events, 20.1 us)
Async XLA Ops:
  0.6 8.1 %collective-permute-start = (bf16[48,2048]{1,0:T(8,128)(2,1)}, bf16[48,2048]{1,0:T(8,128)(2,1)S(1)}, u32[]{:S(2)}, u32[]{:S(2)}) collective-permute-start(bf16[48,2048]{1,0:T(8,128)(2,1)} %param.5), channel_id=1, source_target_pairs={{0,8},{4,12},{8,0},{12,4},{1,9},{5,13},{9,1},{13,5},{2,10},{6,14},... | collective-permute-start | bytes 589832 | tf_op jit(solution)/shard_map/ppermute | solution.py:52
  3.7 8.4 %collective-permute-start.4 = (bf16[48,2048]{1,0:T(8,128)(2,1)}, bf16[48,2048]{1,0:T(8,128)(2,1)S(1)}, u32[]{:S(2)}, u32[]{:S(2)}) collective-permute-start(bf16[48,2048]{1,0:T(8,128)(2,1)} %param.5), channel_id=1, source_target_pairs={{0,4},{4,0},{8,12},{12,8},{1,5},{5,1},{9,13},{13,9},{2,6},{6,2},{1... | collective-permute-start | bytes 589832 | tf_op jit(solution)/shard_map/ppermute | solution.py:253
  8.8 29.3 %collective-permute-start.1 = (bf16[48,2048]{1,0:T(8,128)(2,1)}, bf16[48,2048]{1,0:T(8,128)(2,1)S(1)}, u32[]{:S(2)}, u32[]{:S(2)}) collective-permute-start(bf16[48,2048]{1,0:T(8,128)(2,1)} %param.9), channel_id=1, source_target_pairs={{0,8},{4,12},{8,0},{12,4},{1,9},{5,13},{9,1},{13,5},{2,10},{6,14},... | collective-permute-start | bytes 589832 | tf_op jit(solution)/shard_map/ppermute | solution.py:52
  11.5 26.7 %collective-permute-start.2 = (bf16[48,2048]{1,0:T(8,128)(2,1)}, bf16[48,2048]{1,0:T(8,128)(2,1)S(1)}, u32[]{:S(2)}, u32[]{:S(2)}) collective-permute-start(bf16[48,2048]{1,0:T(8,128)(2,1)} %param.9), channel_id=1, source_target_pairs={{0,4},{4,0},{8,12},{12,8},{1,5},{5,1},{9,13},{13,9},{2,6},{6,2},{1... | collective-permute-start | bytes 589832 | tf_op jit(solution)/shard_map/ppermute | solution.py:253
  11.6 1.7 collective-permute-start.5
  19.1 36.3 %collective-permute-start.8 = (bf16[192,896]{1,0:T(8,128)(2,1)S(1)}, bf16[192,896]{1,0:T(8,128)(2,1)S(1)}, u32[]{:S(2)}, u32[]{:S(2)}) collective-permute-start(bf16[192,896]{1,0:T(8,128)(2,1)S(1)} %bitcast.55), channel_id=1, source_target_pairs={{0,1},{1,3},{3,2},{2,0},{4,5},{5,7},{7,6},{6,4},{8,9},{9,11},{11,1... | collective-permute-start | bytes 1032200 | tf_op jit(solution)/shard_map/ppermute | solution.py:265
  20.7 35.1 %collective-permute-start.11 = (bf16[192,896]{1,0:T(8,128)(2,1)S(1)}, bf16[192,896]{1,0:T(8,128)(2,1)S(1)}, u32[]{:S(2)}, u32[]{:S(2)}) collective-permute-start(bf16[192,896]{1,0:T(8,128)(2,1)S(1)} %bitcast.54), channel_id=1, source_target_pairs={{0,1},{1,3},{3,2},{2,0},{4,5},{5,7},{7,6},{6,4},{8,9},{9,11},{11,1... | collective-permute-start | bytes 1032200 | tf_op jit(solution)/shard_map/ppermute | solution.py:265
  38.1 1.5 collective-permute-start.3
  54.8 11.9 %collective-permute-start.6 = (bf16[192,896]{1,0:T(8,128)(2,1)S(1)}, bf16[192,896]{1,0:T(8,128)(2,1)S(1)}, u32[]{:S(2)}, u32[]{:S(2)}) collective-permute-start(bf16[192,896]{1,0:T(8,128)(2,1)S(1)} %fusion.11), channel_id=1, source_target_pairs={{0,1},{1,3},{3,2},{2,0},{4,5},{5,7},{7,6},{6,4},{8,9},{9,11},{11,1... | collective-permute-start | bytes 1032200 | tf_op jit(solution)/shard_map/ppermute | solution.py:265
  55.4 18.7 %collective-permute-start.9 = (bf16[192,896]{1,0:T(8,128)(2,1)S(1)}, bf16[192,896]{1,0:T(8,128)(2,1)S(1)}, u32[]{:S(2)}, u32[]{:S(2)}) collective-permute-start(bf16[192,896]{1,0:T(8,128)(2,1)S(1)} %fusion.8), channel_id=1, source_target_pairs={{0,1},{1,3},{3,2},{2,0},{4,5},{5,7},{7,6},{6,4},{8,9},{9,11},{11,1... | collective-permute-start | bytes 1032200 | tf_op jit(solution)/shard_map/ppermute | solution.py:265
  55.8 25.6 %collective-permute-start.12 = (bf16[192,896]{1,0:T(8,128)(2,1)S(1)}, bf16[192,896]{1,0:T(8,128)(2,1)S(1)}, u32[]{:S(2)}, u32[]{:S(2)}) collective-permute-start(bf16[192,896]{1,0:T(8,128)(2,1)S(1)} %fusion.6), channel_id=1, source_target_pairs={{0,1},{1,3},{3,2},{2,0},{4,5},{5,7},{7,6},{6,4},{8,9},{9,11},{11,1... | collective-permute-start | bytes 1032200 | tf_op jit(solution)/shard_map/ppermute | solution.py:265
  66.7 22.1 %collective-permute-start.7 = (bf16[192,896]{1,0:T(8,128)(2,1)S(1)}, bf16[192,896]{1,0:T(8,128)(2,1)S(1)}, u32[]{:S(2)}, u32[]{:S(2)}) collective-permute-start(bf16[192,896]{1,0:T(8,128)(2,1)S(1)} %fusion.4), channel_id=1, source_target_pairs={{0,1},{1,3},{3,2},{2,0},{4,5},{5,7},{7,6},{6,4},{8,9},{9,11},{11,1... | collective-permute-start | bytes 1032200 | tf_op jit(solution)/shard_map/ppermute | solution.py:265
  74.1 22.1 %collective-permute-start.10 = (bf16[192,896]{1,0:T(8,128)(2,1)S(1)}, bf16[192,896]{1,0:T(8,128)(2,1)S(1)}, u32[]{:S(2)}, u32[]{:S(2)}) collective-permute-start(bf16[192,896]{1,0:T(8,128)(2,1)S(1)} %fusion.7), channel_id=1, source_target_pairs={{0,1},{1,3},{3,2},{2,0},{4,5},{5,7},{7,6},{6,4},{8,9},{9,11},{11,1... | collective-permute-start | bytes 1032200 | tf_op jit(solution)/shard_map/ppermute | solution.py:265
  81.5 21.3 %collective-permute-start.13 = (bf16[192,896]{1,0:T(8,128)(2,1)S(1)}, bf16[192,896]{1,0:T(8,128)(2,1)S(1)}, u32[]{:S(2)}, u32[]{:S(2)}) collective-permute-start(bf16[192,896]{1,0:T(8,128)(2,1)S(1)} %fusion.5), channel_id=1, source_target_pairs={{0,1},{1,3},{3,2},{2,0},{4,5},{5,7},{7,6},{6,4},{8,9},{9,11},{11,1... | collective-permute-start | bytes 1032200 | tf_op jit(solution)/shard_map/ppermute | solution.py:265
  103.0 11.9 %collective-permute-start.14 = (bf16[192,896]{1,0:T(8,128)(2,1)S(1)}, bf16[192,896]{1,0:T(8,128)(2,1)S(1)}, u32[]{:S(2)}, u32[]{:S(2)}) collective-permute-start(bf16[192,896]{1,0:T(8,128)(2,1)S(1)} %multiply_convert_fusion.2.hidden), channel_id=1, source_target_pairs={{0,1},{1,3},{3,2},{2,0},{4,5},{5,7},{7,6},{6,4},{8,9},{9,11},{11,1... | collective-permute-start | bytes 1032200 | tf_op jit(solution)/shard_map/ppermute | solution.py:265
  103.1 19.3 %collective-permute-start.19 = (bf16[192,896]{1,0:T(8,128)(2,1)S(1)}, bf16[192,896]{1,0:T(8,128)(2,1)S(1)}, u32[]{:S(2)}, u32[]{:S(2)}) collective-permute-start(bf16[192,896]{1,0:T(8,128)(2,1)S(1)} %fusion.2), channel_id=1, source_target_pairs={{0,1},{1,3},{3,2},{2,0},{4,5},{5,7},{7,6},{6,4},{8,9},{9,11},{11,1... | collective-permute-start | bytes 1032200 | tf_op jit(solution)/shard_map/ppermute | solution.py:265
  115.0 15.0 %collective-permute-start.15 = (bf16[192,896]{1,0:T(8,128)(2,1)S(1)}, bf16[192,896]{1,0:T(8,128)(2,1)S(1)}, u32[]{:S(2)}, u32[]{:S(2)}) collective-permute-start(bf16[192,896]{1,0:T(8,128)(2,1)S(1)} %collective-permute-done.14.hidden), channel_id=1, source_target_pairs={{0,1},{1,3},{3,2},{2,0},{4,5},{5,7},{7,6},{6,4},{8,9},{9,11},{11,1... | collective-permute-start | bytes 1032200 | tf_op jit(solution)/shard_map/ppermute | solution.py:265
  122.8 22.0 %collective-permute-start.22 = (bf16[192,896]{1,0:T(8,128)(2,1)S(1)}, bf16[192,896]{1,0:T(8,128)(2,1)S(1)}, u32[]{:S(2)}, u32[]{:S(2)}) collective-permute-start(bf16[192,896]{1,0:T(8,128)(2,1)S(1)} %get-tuple-element.89.pre_up), channel_id=1, source_target_pairs={{0,1},{1,3},{3,2},{2,0},{4,5},{5,7},{7,6},{6,4},{8,9},{9,11},{11,1... | collective-permute-start | bytes 1032200 | tf_op jit(solution)/shard_map/ppermute | solution.py:265
  122.9 25.4 %collective-permute-start.20 = (bf16[192,896]{1,0:T(8,128)(2,1)S(1)}, bf16[192,896]{1,0:T(8,128)(2,1)S(1)}, u32[]{:S(2)}, u32[]{:S(2)}) collective-permute-start(bf16[192,896]{1,0:T(8,128)(2,1)S(1)} %get-tuple-element.90.pre_gate), channel_id=1, source_target_pairs={{0,1},{1,3},{3,2},{2,0},{4,5},{5,7},{7,6},{6,4},{8,9},{9,11},{11,1... | collective-permute-start | bytes 1032200 | tf_op jit(solution)/shard_map/ppermute | solution.py:265
  130.0 24.7 %collective-permute-start.16 = (bf16[192,896]{1,0:T(8,128)(2,1)S(1)}, bf16[192,896]{1,0:T(8,128)(2,1)S(1)}, u32[]{:S(2)}, u32[]{:S(2)}) collective-permute-start(bf16[192,896]{1,0:T(8,128)(2,1)S(1)} %collective-permute-done.15.hidden), channel_id=1, source_target_pairs={{0,1},{1,3},{3,2},{2,0},{4,5},{5,7},{7,6},{6,4},{8,9},{9,11},{11,1... | collective-permute-start | bytes 1032200 | tf_op jit(solution)/shard_map/ppermute | solution.py:265
  144.8 30.5 %collective-permute-start.24 = (bf16[192,896]{1,0:T(8,128)(2,1)S(1)}, bf16[192,896]{1,0:T(8,128)(2,1)S(1)}, u32[]{:S(2)}, u32[]{:S(2)}) collective-permute-start(bf16[192,896]{1,0:T(8,128)(2,1)S(1)} %collective-permute-done.22.pre_up), channel_id=1, source_target_pairs={{0,1},{1,3},{3,2},{2,0},{4,5},{5,7},{7,6},{6,4},{8,9},{9,11},{11,1... | collective-permute-start | bytes 1032200 | tf_op jit(solution)/shard_map/ppermute | solution.py:265
  148.2 27.0 %collective-permute-start.21 = (bf16[192,896]{1,0:T(8,128)(2,1)S(1)}, bf16[192,896]{1,0:T(8,128)(2,1)S(1)}, u32[]{:S(2)}, u32[]{:S(2)}) collective-permute-start(bf16[192,896]{1,0:T(8,128)(2,1)S(1)} %collective-permute-done.20.pre_gate), channel_id=1, source_target_pairs={{0,1},{1,3},{3,2},{2,0},{4,5},{5,7},{7,6},{6,4},{8,9},{9,11},{11,1... | collective-permute-start | bytes 1032200 | tf_op jit(solution)/shard_map/ppermute | solution.py:265
  161.1 53.6 %collective-permute-start.17 = (f32[96,2048]{1,0:T(8,128)S(1)}, f32[96,2048]{1,0:T(8,128)S(1)}, u32[]{:S(2)}, u32[]{:S(2)}) collective-permute-start(f32[96,2048]{1,0:T(8,128)S(1)} %slice.93), channel_id=1, source_target_pairs={{0,4},{4,0},{8,12},{12,8},{1,5},{5,1},{9,13},{13,9},{2,6},{6,2},{1... | collective-permute-start | bytes 2359304 | tf_op jit(solution)/shard_map/ppermute | solution.py:257
  175.3 11.9 %collective-permute-start.25 = (bf16[192,896]{1,0:T(8,128)(2,1)S(1)}, bf16[192,896]{1,0:T(8,128)(2,1)S(1)}, u32[]{:S(2)}, u32[]{:S(2)}) collective-permute-start(bf16[192,896]{1,0:T(8,128)(2,1)S(1)} %collective-permute-done.24.pre_up), channel_id=1, source_target_pairs={{0,1},{1,3},{3,2},{2,0},{4,5},{5,7},{7,6},{6,4},{8,9},{9,11},{11,1... | collective-permute-start | bytes 1032200 | tf_op jit(solution)/shard_map/ppermute | solution.py:265
  176.0 18.3 %collective-permute-start.23 = (bf16[192,896]{1,0:T(8,128)(2,1)S(1)}, bf16[192,896]{1,0:T(8,128)(2,1)S(1)}, u32[]{:S(2)}, u32[]{:S(2)}) collective-permute-start(bf16[192,896]{1,0:T(8,128)(2,1)S(1)} %collective-permute-done.21.pre_gate), channel_id=1, source_target_pairs={{0,1},{1,3},{3,2},{2,0},{4,5},{5,7},{7,6},{6,4},{8,9},{9,11},{11,1... | collective-permute-start | bytes 1032200 | tf_op jit(solution)/shard_map/ppermute | solution.py:265
  202.2 13.2 %collective-permute-start.26 = (f32[96,2048]{1,0:T(8,128)S(1)}, f32[96,2048]{1,0:T(8,128)S(1)}, u32[]{:S(2)}, u32[]{:S(2)}) collective-permute-start(f32[96,2048]{1,0:T(8,128)S(1)} %slice.108), channel_id=1, source_target_pairs={{0,4},{4,0},{8,12},{12,8},{1,5},{5,1},{9,13},{13,9},{2,6},{6,2},{1... | collective-permute-start | bytes 2359304 | tf_op jit(solution)/shard_map/ppermute | solution.py:257
  214.8 7.8 %collective-permute-start.18 = (bf16[48,2048]{1,0:T(8,128)(2,1)S(1)}, bf16[48,2048]{1,0:T(8,128)(2,1)S(1)}, u32[]{:S(2)}, u32[]{:S(2)}) collective-permute-start(bf16[48,2048]{1,0:T(8,128)(2,1)S(1)} %slice.158), channel_id=1, source_target_pairs={{0,8},{4,12},{8,0},{12,4},{1,9},{5,13},{9,1},{13,5},{2,10},{6,14},... | collective-permute-start | bytes 589832 | tf_op jit(solution)/shard_map/ppermute | solution.py:59
  215.5 10.9 %collective-permute-start.27 = (bf16[48,2048]{1,0:T(8,128)(2,1)S(1)}, bf16[48,2048]{1,0:T(8,128)(2,1)S(1)}, u32[]{:S(2)}, u32[]{:S(2)}) collective-permute-start(bf16[48,2048]{1,0:T(8,128)(2,1)S(1)} %slice.157), channel_id=1, source_target_pairs={{0,8},{4,12},{8,0},{12,4},{1,9},{5,13},{9,1},{13,5},{2,10},{6,14},... | collective-permute-start | bytes 589832 | tf_op jit(solution)/shard_map/ppermute | solution.py:59
